TPU v7x, 512 devices: a whole 4x8x8 slice. The times are simulated.
512 devices in a mesh: fsdp: 32 (over z, x), mp: 16 (over y, core).
Axes of the slice: x: 4, y: 8, z: 8, core: 2. Of those that a mesh axis runs over, the one named last changes fastest.
Arguments:
- tokens: bfloat16 [12288, 2048], P('fsdp', 'mp'), may hold values from -6 to 6
- cotangent: bfloat16 [12288, 2048], P('fsdp', 'mp'), may hold values from -6 to 6
- gate_weight: bfloat16 [2048, 6144], P('fsdp', 'mp'), may hold values from -0.125 to 0.125
- up_weight: bfloat16 [2048, 6144], P('fsdp', 'mp'), may hold values from -0.125 to 0.125
- down_weight: bfloat16 [2048, 6144], P('fsdp', 'mp'), may hold values from -0.125 to 0.125
Outputs:
- input_grad: bfloat16 [12288, 2048], P('fsdp', 'mp')
- grad_down: bfloat16 [2048, 6144], P('fsdp', 'mp')
All inputs are finite; a program needn't handle non-finite values.
Results may differ from a plain program's by a relative error of at most 0.022.
Values may be sent and summed in bfloat16 or wider, within the bound.
No kernel may reach another device: no remote copies, remote signals or barrier semaphores. Data moves between devices by JAX's collectives and lax.ppermute only.
A program may use at most 64 MiB of HBM per device.

v0:
```python
import math

import jax
import jax.numpy as jnp
from jax import lax
from jax.sharding import PartitionSpec as P

N_Z = 8
N_X = 4
N_Y = 8
N_CORE = 2
Z_GROUPS = [[z * N_X + x for z in range(N_Z)] for x in range(N_X)]
Y_GROUPS = [[y * N_CORE + c for y in range(N_Y)] for c in range(N_CORE)]


def dot(left, right, dims):
    return lax.dot_general(left, right, (dims, ((), ())), preferred_element_type=jnp.float32)


def send_x(value, step):
    pairs = [
        (z * N_X + x, z * N_X + (x + step) % N_X) for z in range(N_Z) for x in range(N_X)
    ]
    return lax.ppermute(value, "fsdp", pairs)


def send_core(value):
    pairs = [(i, i ^ 1) for i in range(N_Y * N_CORE)]
    return lax.ppermute(value, "mp", pairs)


def gather_z(block):
    copies = jnp.broadcast_to(block[None], (N_Z,) + block.shape)
    return lax.all_to_all(copies, "fsdp", 0, 0, axis_index_groups=Z_GROUPS)


def gather_x(own, me):
    half = N_Z // 2
    from_left = send_x(own, 1)
    from_right = send_x(own, -1)
    far_low = send_x(from_left[:half], 1)
    far_high = send_x(from_right[half:], -1)
    full = jnp.zeros((N_Z, N_X) + own.shape[1:], own.dtype)
    left, right, far = (me + N_X - 1) % N_X, (me + 1) % N_X, (me + 2) % N_X
    put = lambda into, block, z, x: lax.dynamic_update_slice(into, block[:, None], (z, x, 0, 0))
    full = put(full, own, 0, me)
    full = put(full, from_left, 0, left)
    full = put(full, from_right, 0, right)
    full = put(full, far_low, 0, far)
    full = put(full, far_high, half, far)
    return full


def add(left, right):
    return left.astype(jnp.float32) + right.astype(jnp.float32)


def scatter_x(partial_value, me):
    half = N_Z // 2
    take = lambda x, lo, hi: lax.dynamic_index_in_dim(partial_value, x, 1, keepdims=False)[lo:hi]
    left, right, far = (me + N_X - 1) % N_X, (me + 1) % N_X, (me + 2) % N_X
    low = send_x(take(far, 0, half), 1)
    high = send_x(take(far, half, N_Z), -1)
    to_right = jnp.concatenate(
        [add(take(right, 0, half), low).astype(jnp.bfloat16), take(right, half, N_Z)]
    )
    to_left = jnp.concatenate(
        [take(left, 0, half), add(take(left, half, N_Z), high).astype(jnp.bfloat16)]
    )
    from_left = send_x(to_right, 1)
    from_right = send_x(to_left, -1)
    return add(take(me, 0, N_Z), from_left) + from_right.astype(jnp.float32)


def on_device(tokens, cotangent, gate_weight, up_weight, down_weight):
    n_fsdp = lax.axis_size("fsdp")
    rows, width = tokens.shape
    depth, cols = gate_weight.shape
    factor = 1.0 / math.sqrt(rows * n_fsdp)
    me_x = lax.axis_index("fsdp") % N_X
    core = lax.axis_index("mp") % N_CORE

    stacked = jnp.concatenate([tokens, cotangent])
    gathered = lax.all_gather(stacked, "mp", axis=1, tiled=True)
    token_rows, cotangent_rows = gathered[:rows], gathered[rows:]

    gate_up = gather_x(gather_z(jnp.concatenate([gate_weight, up_weight])), me_x)
    gate_full = gate_up[:, :, :depth].reshape(-1, cols)
    up_full = gate_up[:, :, depth:].reshape(-1, cols)
    down_full = gather_x(gather_z(down_weight), me_x).reshape(-1, cols)

    gate_value = dot(token_rows, gate_full, ((1,), (0,)))
    up_value = dot(token_rows, up_full, ((1,), (0,)))
    sigmoid_gate = jax.nn.sigmoid(gate_value)
    hidden = (gate_value * sigmoid_gate * up_value).astype(jnp.bfloat16)

    down_partial = dot(cotangent_rows, hidden, ((0,), (0,))).astype(jnp.bfloat16)
    down_x = scatter_x(down_partial.reshape(N_Z, N_X, depth, cols), me_x)
    down_z = lax.all_to_all(
        down_x.astype(jnp.bfloat16), "fsdp", 0, 0, axis_index_groups=Z_GROUPS
    )
    grad_down = (down_z.astype(jnp.float32).sum(0) * factor).astype(jnp.bfloat16)

    hidden_grad = dot(cotangent_rows, down_full, ((1,), (0,)))
    gate_grad = (
        hidden_grad * up_value * sigmoid_gate * (1.0 + gate_value * (1.0 - sigmoid_gate))
    ).astype(jnp.bfloat16)
    up_grad = (hidden_grad * gate_value * sigmoid_gate).astype(jnp.bfloat16)
    partial_value = (
        dot(gate_grad, gate_full, ((1,), (1,))) + dot(up_grad, up_full, ((1,), (1,)))
    ).astype(jnp.bfloat16)
    blocks = partial_value.reshape(rows, N_Y, N_CORE, width).transpose(2, 1, 0, 3)
    mine = lax.dynamic_index_in_dim(blocks, core, 0, keepdims=False)
    other = lax.dynamic_index_in_dim(blocks, 1 - core, 0, keepdims=False)
    pair_sum = add(mine, send_core(other)).astype(jnp.bfloat16)
    summed = lax.all_to_all(pair_sum, "mp", 0, 0, axis_index_groups=Y_GROUPS)
    input_grad = summed.astype(jnp.float32).sum(0).astype(jnp.bfloat16)
    return (input_grad, grad_down)


def solution(mesh):
    placed = P("fsdp", "mp")
    return jax.shard_map(
        on_device,
        mesh=mesh,
        in_specs=(placed,) * 5,
        out_specs=(placed, placed),
        check_vma=False,
    )
```

profile of v0, /device:TPU:6, one launch (start us, length us, event | category | flops | bytes accessed | tf_op | source)
XLA Modules:
  0.0 195.8 jit_solution(8532763815374037181)
XLA Ops:
  10.5 10.3 %all-to-all-start = ((bf16[8,64,384]{2,1,0:T(8,128)(2,1)}), bf16[8,64,384]{2,1,0:T(8,128)(2,1)S(1)}, u32[]{:S(2)}, u32[]{:S(2)}) async-start(bf16[8,64,384]{2,1,0:T(8,128)(2,1)} %broadcast_in_dim.49), calls=%async_computation | async-start | bytes 786432 | tf_op jit(solution)/shard_map/all_to_all | solution.py:34
  20.8 14.7 %all-to-all-done = bf16[8,64,384]{2,1,0:T(8,128)(2,1)S(1)} async-done(((bf16[8,64,384]{2,1,0:T(8,128)(2,1)}), bf16[8,64,384]{2,1,0:T(8,128)(2,1)S(1)}, u32[]{:S(2)}, u32[]{:S(2)}) %all-to-all-start) | async-done | bytes 393248 | tf_op jit(solution)/shard_map/all_to_all | solution.py:34
  36.4 3.5 %all-to-all-start.1 = ((bf16[8,128,384]{2,1,0:T(8,128)(2,1)}), bf16[8,128,384]{2,1,0:T(8,128)(2,1)S(1)}, u32[]{:S(2)}, u32[]{:S(2)}) async-start(bf16[8,128,384]{2,1,0:T(8,128)(2,1)} %broadcast_in_dim.56), calls=%async_computation.1 | async-start | bytes 1572864 | tf_op jit(solution)/shard_map/all_to_all | solution.py:34
  40.0 2.4 %collective-permute-start = (bf16[8,64,384]{2,1,0:T(8,128)(2,1)S(1)}, bf16[8,64,384]{2,1,0:T(8,128)(2,1)S(1)}, u32[]{:S(2)}, u32[]{:S(2)}) collective-permute-start(bf16[8,64,384]{2,1,0:T(8,128)(2,1)S(1)} %all-to-all-done), channel_id=1, source_target_pairs={{0,16},{16,32},{32,48},{48,0},{64,80},{80,96},{96,112},{112,64},{1... | collective-permute-start | bytes 1179656 | tf_op jit(solution)/shard_map/ppermute | solution.py:24
  42.4 3.5 %collective-permute-start.1 = (bf16[8,64,384]{2,1,0:T(8,128)(2,1)S(1)}, bf16[8,64,384]{2,1,0:T(8,128)(2,1)S(1)}, u32[]{:S(2)}, u32[]{:S(2)}) collective-permute-start(bf16[8,64,384]{2,1,0:T(8,128)(2,1)S(1)} %all-to-all-done), channel_id=1, source_target_pairs={{0,48},{16,0},{32,16},{48,32},{64,112},{80,64},{96,80},{112,96},{1... | collective-permute-start | bytes 1179656 | tf_op jit(solution)/shard_map/ppermute | solution.py:24
  46.2 5.7 %collective-permute-done = bf16[8,64,384]{2,1,0:T(8,128)(2,1)S(1)} collective-permute-done((bf16[8,64,384]{2,1,0:T(8,128)(2,1)S(1)}, bf16[8,64,384]{2,1,0:T(8,128)(2,1)S(1)}, u32[]{:S(2)}, u32[]{:S(2)}) %collective-permute-start) | collective-permute-done | bytes 393248 | tf_op jit(solution)/shard_map/ppermute | solution.py:24
  52.6 3.6 %collective-permute-start.2 = (bf16[4,64,384]{2,1,0:T(8,128)(2,1)}, bf16[4,64,384]{2,1,0:T(8,128)(2,1)}, u32[]{:S(2)}, u32[]{:S(2)}) collective-permute-start(bf16[4,64,384]{2,1,0:T(8,128)(2,1)} %slice.75), channel_id=1, source_target_pairs={{0,16},{16,32},{32,48},{48,0},{64,80},{80,96},{96,112},{112,64},{1... | collective-permute-start | bytes 589832 | tf_op jit(solution)/shard_map/ppermute | solution.py:24
  58.6 3.9 %all-to-all-done.1 = bf16[8,128,384]{2,1,0:T(8,128)(2,1)S(1)} async-done(((bf16[8,128,384]{2,1,0:T(8,128)(2,1)}), bf16[8,128,384]{2,1,0:T(8,128)(2,1)S(1)}, u32[]{:S(2)}, u32[]{:S(2)}) %all-to-all-start.1) | async-done | bytes 786464 | tf_op jit(solution)/shard_map/all_to_all | solution.py:34
  62.5 2.4 %collective-permute-start.4 = (bf16[8,128,384]{2,1,0:T(8,128)(2,1)S(1)}, bf16[8,128,384]{2,1,0:T(8,128)(2,1)S(1)}, u32[]{:S(2)}, u32[]{:S(2)}) collective-permute-start(bf16[8,128,384]{2,1,0:T(8,128)(2,1)S(1)} %all-to-all-done.1), channel_id=1, source_target_pairs={{0,16},{16,32},{32,48},{48,0},{64,80},{80,96},{96,112},{112,64},{1... | collective-permute-start | bytes 2359304 | tf_op jit(solution)/shard_map/ppermute | solution.py:24
  64.9 3.5 %collective-permute-start.5 = (bf16[8,128,384]{2,1,0:T(8,128)(2,1)S(1)}, bf16[8,128,384]{2,1,0:T(8,128)(2,1)S(1)}, u32[]{:S(2)}, u32[]{:S(2)}) collective-permute-start(bf16[8,128,384]{2,1,0:T(8,128)(2,1)S(1)} %all-to-all-done.1), channel_id=1, source_target_pairs={{0,48},{16,0},{32,16},{48,32},{64,112},{80,64},{96,80},{112,96},{1... | collective-permute-start | bytes 2359304 | tf_op jit(solution)/shard_map/ppermute | solution.py:24
  70.1 13.7 %collective-permute-done.4 = bf16[8,128,384]{2,1,0:T(8,128)(2,1)S(1)} collective-permute-done((bf16[8,128,384]{2,1,0:T(8,128)(2,1)S(1)}, bf16[8,128,384]{2,1,0:T(8,128)(2,1)S(1)}, u32[]{:S(2)}, u32[]{:S(2)}) %collective-permute-start.4) | collective-permute-done | bytes 786464 | tf_op jit(solution)/shard_map/ppermute | solution.py:24
  83.9 3.6 %collective-permute-start.6 = (bf16[4,128,384]{2,1,0:T(8,128)(2,1)S(1)}, bf16[4,128,384]{2,1,0:T(8,128)(2,1)S(1)}, u32[]{:S(2)}, u32[]{:S(2)}) collective-permute-start(bf16[4,128,384]{2,1,0:T(8,128)(2,1)S(1)} %slice.78), channel_id=1, source_target_pairs={{0,16},{16,32},{32,48},{48,0},{64,80},{80,96},{96,112},{112,64},{1... | collective-permute-start | bytes 1179656 | tf_op jit(solution)/shard_map/ppermute | solution.py:24
  90.1 5.8 %collective-permute-done.6 = bf16[4,128,384]{2,1,0:T(8,128)(2,1)S(1)} collective-permute-done((bf16[4,128,384]{2,1,0:T(8,128)(2,1)S(1)}, bf16[4,128,384]{2,1,0:T(8,128)(2,1)S(1)}, u32[]{:S(2)}, u32[]{:S(2)}) %collective-permute-start.6) | collective-permute-done | bytes 393248 | tf_op jit(solution)/shard_map/ppermute | solution.py:24
  96.0 4.5 %collective-permute-done.7 = bf16[4,128,384]{2,1,0:T(8,128)(2,1)S(1)} collective-permute-done((bf16[4,128,384]{2,1,0:T(8,128)(2,1)S(1)}, bf16[4,128,384]{2,1,0:T(8,128)(2,1)S(1)}, u32[]{:S(2)}, u32[]{:S(2)}) %collective-permute-start.7) | collective-permute-done | bytes 393248 | tf_op jit(solution)/shard_map/ppermute | solution.py:24
  101.1 3.4 %fusion.6 = f32[384,384]{1,0:T(8,128)S(1)} fusion(bf16[2048,384]{1,0:T(8,128)(2,1)} %bitcast.99, bf16[768,2048]{1,0:T(8,128)(2,1)} %all-gather.2.cloned.1.call-done), kind=kOutput, calls=%fused_computation.9 | convolution fusion | flops 603979776 | bytes 3735552 | tf_op jit(solution)/shard_map/dot_general | solution.py:17
  110.9 4.1 %collective-permute-start.11 = (bf16[4,64,384]{2,1,0:T(8,128)(2,1)S(1)}, bf16[4,64,384]{2,1,0:T(8,128)(2,1)S(1)}, u32[]{:S(2)}, u32[]{:S(2)}) collective-permute-start(bf16[4,64,384]{2,1,0:T(8,128)(2,1)S(1)} %get-tuple-element.8), channel_id=1, source_target_pairs={{0,48},{16,0},{32,16},{48,32},{64,112},{80,64},{96,80},{112,96},{1... | collective-permute-start | bytes 589832 | tf_op jit(solution)/shard_map/ppermute | solution.py:24
  116.5 3.3 %collective-permute-done.11 = bf16[4,64,384]{2,1,0:T(8,128)(2,1)S(1)} collective-permute-done((bf16[4,64,384]{2,1,0:T(8,128)(2,1)S(1)}, bf16[4,64,384]{2,1,0:T(8,128)(2,1)S(1)}, u32[]{:S(2)}, u32[]{:S(2)}) %collective-permute-start.11) | collective-permute-done | bytes 196640 | tf_op jit(solution)/shard_map/ppermute | solution.py:24
  120.0 2.7 %collective-permute-start.12 = (bf16[8,64,384]{2,1,0:T(8,128)(2,1)S(1)}, bf16[8,64,384]{2,1,0:T(8,128)(2,1)}, u32[]{:S(2)}, u32[]{:S(2)}) collective-permute-start(bf16[8,64,384]{2,1,0:T(8,128)(2,1)S(1)} %pad_maximum_fusion.1), channel_id=1, source_target_pairs={{0,48},{16,0},{32,16},{48,32},{64,112},{80,64},{96,80},{112,96},{1... | collective-permute-start | bytes 1179656 | tf_op jit(solution)/shard_map/ppermute | solution.py:24
  123.5 4.5 %collective-permute-start.10 = (bf16[8,64,384]{2,1,0:T(8,128)(2,1)}, bf16[8,64,384]{2,1,0:T(8,128)(2,1)}, u32[]{:S(2)}, u32[]{:S(2)}) collective-permute-start(bf16[8,64,384]{2,1,0:T(8,128)(2,1)} %pad_maximum_fusion), channel_id=1, source_target_pairs={{0,16},{16,32},{32,48},{48,0},{64,80},{80,96},{96,112},{112,64},{1... | collective-permute-start | bytes 1179656 | tf_op jit(solution)/shard_map/ppermute | solution.py:24
  130.3 3.2 %constant_dynamic-slice_fusion.1 = (bf16[384,8,1,128]{3,2,1,0:T(2,128)(2,1)S(1)}, bf16[384,8,1,128]{3,2,1,0:T(2,128)(2,1)S(1)}) fusion(bf16[384,8,2,128]{3,2,1,0:T(2,128)(2,1)S(1)} %reshape.38, s32[]{:T(128)S(6)} %select_n.77, s32[]{:T(128)S(6)} %select_n.78), kind=kLoop, calls=%fused_computation.51 | loop fusion | bytes 3145736 | tf_op jit(solution)/shard_map/jit(dynamic_index_in_dim)/dynamic_slice | solution.py:113
  138.8 3.5 %all-to-all-start.3 = ((bf16[8,64,384]{2,1,0:T(8,128)(2,1)}), bf16[8,64,384]{2,1,0:T(8,128)(2,1)S(1)}, u32[]{:S(2)}, u32[]{:S(2)}) async-start(bf16[8,64,384]{2,1,0:T(8,128)(2,1)} %fusion.9), calls=%async_computation.3 | async-start | bytes 786432 | tf_op jit(solution)/shard_map/all_to_all | solution.py:99
  143.5 14.3 %all-to-all-done.3 = bf16[8,64,384]{2,1,0:T(8,128)(2,1)S(1)} async-done(((bf16[8,64,384]{2,1,0:T(8,128)(2,1)}), bf16[8,64,384]{2,1,0:T(8,128)(2,1)S(1)}, u32[]{:S(2)}, u32[]{:S(2)}) %all-to-all-start.3) | async-done | bytes 393248 | tf_op jit(solution)/shard_map/all_to_all | solution.py:99
  157.8 7.1 %all-to-all-start.2 = ((bf16[8,384,128]{2,1,0:T(8,128)(2,1)}), bf16[8,384,128]{2,1,0:T(8,128)(2,1)S(1)}, u32[]{:S(2)}, u32[]{:S(2)}) async-start(bf16[8,384,128]{2,1,0:T(8,128)(2,1)} %fusion), calls=%async_computation.2 | async-start | bytes 1572864 | tf_op jit(solution)/shard_map/all_to_all | solution.py:116
  165.6 22.7 %all-to-all-done.2 = bf16[8,384,128]{2,1,0:T(8,128)(2,1)S(1)} async-done(((bf16[8,384,128]{2,1,0:T(8,128)(2,1)}), bf16[8,384,128]{2,1,0:T(8,128)(2,1)S(1)}, u32[]{:S(2)}, u32[]{:S(2)}) %all-to-all-start.2) | async-done | bytes 786464 | tf_op jit(solution)/shard_map/all_to_all | solution.py:116
  (68 shorter events, 31.4 us)
Async XLA Ops:
  7.2 13.6 %copy-start.4 = (bf16[64,384]{1,0:T(8,128)(2,1)S(1)}, bf16[64,384]{1,0:T(8,128)(2,1)}, u32[]{:S(2)}) copy-start(bf16[64,384]{1,0:T(8,128)(2,1)} %param.8) | copy-start | bytes 147460
  7.2 13.6 %copy-start.5 = (bf16[64,384]{1,0:T(8,128)(2,1)S(1)}, bf16[64,384]{1,0:T(8,128)(2,1)}, u32[]{:S(2)}) copy-start(bf16[64,384]{1,0:T(8,128)(2,1)} %param.7) | copy-start | bytes 147460
  7.2 93.9 %all-gather.2.cloned.1.call-start = ((), (), s32[]{:S(2)}) async-start(), calls=%async_computation.4 | async-start | bytes 3342336 | tf_op jit(solution)/shard_map/all_gather | solution.py:84
  10.5 25.0 %all-to-all-start = ((bf16[8,64,384]{2,1,0:T(8,128)(2,1)}), bf16[8,64,384]{2,1,0:T(8,128)(2,1)S(1)}, u32[]{:S(2)}, u32[]{:S(2)}) async-start(bf16[8,64,384]{2,1,0:T(8,128)(2,1)} %broadcast_in_dim.49), calls=%async_computation | async-start | bytes 786432 | tf_op jit(solution)/shard_map/all_to_all | solution.py:34
  36.4 26.1 %all-to-all-start.1 = ((bf16[8,128,384]{2,1,0:T(8,128)(2,1)}), bf16[8,128,384]{2,1,0:T(8,128)(2,1)S(1)}, u32[]{:S(2)}, u32[]{:S(2)}) async-start(bf16[8,128,384]{2,1,0:T(8,128)(2,1)} %broadcast_in_dim.56), calls=%async_computation.1 | async-start | bytes 1572864 | tf_op jit(solution)/shard_map/all_to_all | solution.py:34
  40.0 12.0 %collective-permute-start = (bf16[8,64,384]{2,1,0:T(8,128)(2,1)S(1)}, bf16[8,64,384]{2,1,0:T(8,128)(2,1)S(1)}, u32[]{:S(2)}, u32[]{:S(2)}) collective-permute-start(bf16[8,64,384]{2,1,0:T(8,128)(2,1)S(1)} %all-to-all-done), channel_id=1, source_target_pairs={{0,16},{16,32},{32,48},{48,0},{64,80},{80,96},{96,112},{112,64},{1... | collective-permute-start | bytes 1179656 | tf_op jit(solution)/shard_map/ppermute | solution.py:24
  42.4 13.9 %collective-permute-start.1 = (bf16[8,64,384]{2,1,0:T(8,128)(2,1)S(1)}, bf16[8,64,384]{2,1,0:T(8,128)(2,1)S(1)}, u32[]{:S(2)}, u32[]{:S(2)}) collective-permute-start(bf16[8,64,384]{2,1,0:T(8,128)(2,1)S(1)} %all-to-all-done), channel_id=1, source_target_pairs={{0,48},{16,0},{32,16},{48,32},{64,112},{80,64},{96,80},{112,96},{1... | collective-permute-start | bytes 1179656 | tf_op jit(solution)/shard_map/ppermute | solution.py:24
  52.6 15.8 %collective-permute-start.2 = (bf16[4,64,384]{2,1,0:T(8,128)(2,1)}, bf16[4,64,384]{2,1,0:T(8,128)(2,1)}, u32[]{:S(2)}, u32[]{:S(2)}) collective-permute-start(bf16[4,64,384]{2,1,0:T(8,128)(2,1)} %slice.75), channel_id=1, source_target_pairs={{0,16},{16,32},{32,48},{48,0},{64,80},{80,96},{96,112},{112,64},{1... | collective-permute-start | bytes 589832 | tf_op jit(solution)/shard_map/ppermute | solution.py:24
  56.3 13.1 %collective-permute-start.3 = (bf16[4,64,384]{2,1,0:T(8,128)(2,1)S(1)}, bf16[4,64,384]{2,1,0:T(8,128)(2,1)S(1)}, u32[]{:S(2)}, u32[]{:S(2)}) collective-permute-start(bf16[4,64,384]{2,1,0:T(8,128)(2,1)S(1)} %slice.76), channel_id=1, source_target_pairs={{0,48},{16,0},{32,16},{48,32},{64,112},{80,64},{96,80},{112,96},{1... | collective-permute-start | bytes 589832 | tf_op jit(solution)/shard_map/ppermute | solution.py:24
  62.5 21.3 %collective-permute-start.4 = (bf16[8,128,384]{2,1,0:T(8,128)(2,1)S(1)}, bf16[8,128,384]{2,1,0:T(8,128)(2,1)S(1)}, u32[]{:S(2)}, u32[]{:S(2)}) collective-permute-start(bf16[8,128,384]{2,1,0:T(8,128)(2,1)S(1)} %all-to-all-done.1), channel_id=1, source_target_pairs={{0,16},{16,32},{32,48},{48,0},{64,80},{80,96},{96,112},{112,64},{1... | collective-permute-start | bytes 2359304 | tf_op jit(solution)/shard_map/ppermute | solution.py:24
  64.9 22.6 %collective-permute-start.5 = (bf16[8,128,384]{2,1,0:T(8,128)(2,1)S(1)}, bf16[8,128,384]{2,1,0:T(8,128)(2,1)S(1)}, u32[]{:S(2)}, u32[]{:S(2)}) collective-permute-start(bf16[8,128,384]{2,1,0:T(8,128)(2,1)S(1)} %all-to-all-done.1), channel_id=1, source_target_pairs={{0,48},{16,0},{32,16},{48,32},{64,112},{80,64},{96,80},{112,96},{1... | collective-permute-start | bytes 2359304 | tf_op jit(solution)/shard_map/ppermute | solution.py:24
  69.5 20.7 %copy-start.3 = (bf16[8,4,64,384]{3,2,1,0:T(8,128)(2,1)}, bf16[8,4,64,384]{3,2,1,0:T(8,128)(2,1)S(1)}, u32[]{:S(2)}) copy-start(bf16[8,4,64,384]{3,2,1,0:T(8,128)(2,1)S(1)} %bitcast_dynamic-update-slice_fusion.9) | copy-start | bytes 4718596
  83.9 12.1 %collective-permute-start.6 = (bf16[4,128,384]{2,1,0:T(8,128)(2,1)S(1)}, bf16[4,128,384]{2,1,0:T(8,128)(2,1)S(1)}, u32[]{:S(2)}, u32[]{:S(2)}) collective-permute-start(bf16[4,128,384]{2,1,0:T(8,128)(2,1)S(1)} %slice.78), channel_id=1, source_target_pairs={{0,16},{16,32},{32,48},{48,0},{64,80},{80,96},{96,112},{112,64},{1... | collective-permute-start | bytes 1179656 | tf_op jit(solution)/shard_map/ppermute | solution.py:24
  87.6 13.0 %collective-permute-start.7 = (bf16[4,128,384]{2,1,0:T(8,128)(2,1)S(1)}, bf16[4,128,384]{2,1,0:T(8,128)(2,1)S(1)}, u32[]{:S(2)}, u32[]{:S(2)}) collective-permute-start(bf16[4,128,384]{2,1,0:T(8,128)(2,1)S(1)} %slice.79), channel_id=1, source_target_pairs={{0,48},{16,0},{32,16},{48,32},{64,112},{80,64},{96,80},{112,96},{1... | collective-permute-start | bytes 1179656 | tf_op jit(solution)/shard_map/ppermute | solution.py:24
  101.0 3.5 %copy-start = (bf16[8,4,64,384]{3,2,1,0:T(8,128)(2,1)}, bf16[8,4,64,384]{3,2,1,0:T(8,128)(2,1)S(1)}, u32[]{:S(2)}) copy-start(bf16[8,4,64,384]{3,2,1,0:T(8,128)(2,1)S(1)} %get-tuple-element.2) | copy-start | bytes 4718596
  108.8 11.1 %copy-start.2 = (bf16[2048,384]{1,0:T(8,128)(2,1)}, bf16[2048,384]{1,0:T(8,128)(2,1)S(1)}, u32[]{:S(2)}) copy-start(bf16[2048,384]{1,0:T(8,128)(2,1)S(1)} %convolution_convert_fusion) | copy-start | bytes 4718596
  108.9 7.6 %collective-permute-start.9 = (bf16[4,64,384]{2,1,0:T(8,128)(2,1)S(1)}, bf16[4,64,384]{2,1,0:T(8,128)(2,1)S(1)}, u32[]{:S(2)}, u32[]{:S(2)}) collective-permute-start(bf16[4,64,384]{2,1,0:T(8,128)(2,1)S(1)} %get-tuple-element.6), channel_id=1, source_target_pairs={{0,16},{16,32},{32,48},{48,0},{64,80},{80,96},{96,112},{112,64},{1... | collective-permute-start | bytes 589832 | tf_op jit(solution)/shard_map/ppermute | solution.py:24
  110.9 17.1 %copy-start.1 = (bf16[8,4,64,384]{3,2,1,0:T(8,128)(2,1)S(1)}, bf16[8,4,64,384]{3,2,1,0:T(8,128)(2,1)}, u32[]{:S(2)}) copy-start(bf16[8,4,64,384]{3,2,1,0:T(8,128)(2,1)} %copy-done) | copy-start | bytes 4718596
  110.9 8.9 %collective-permute-start.11 = (bf16[4,64,384]{2,1,0:T(8,128)(2,1)S(1)}, bf16[4,64,384]{2,1,0:T(8,128)(2,1)S(1)}, u32[]{:S(2)}, u32[]{:S(2)}) collective-permute-start(bf16[4,64,384]{2,1,0:T(8,128)(2,1)S(1)} %get-tuple-element.8), channel_id=1, source_target_pairs={{0,48},{16,0},{32,16},{48,32},{64,112},{80,64},{96,80},{112,96},{1... | collective-permute-start | bytes 589832 | tf_op jit(solution)/shard_map/ppermute | solution.py:24
  120.0 16.7 %collective-permute-start.12 = (bf16[8,64,384]{2,1,0:T(8,128)(2,1)S(1)}, bf16[8,64,384]{2,1,0:T(8,128)(2,1)}, u32[]{:S(2)}, u32[]{:S(2)}) collective-permute-start(bf16[8,64,384]{2,1,0:T(8,128)(2,1)S(1)} %pad_maximum_fusion.1), channel_id=1, source_target_pairs={{0,48},{16,0},{32,16},{48,32},{64,112},{80,64},{96,80},{112,96},{1... | collective-permute-start | bytes 1179656 | tf_op jit(solution)/shard_map/ppermute | solution.py:24
  123.5 13.2 %collective-permute-start.10 = (bf16[8,64,384]{2,1,0:T(8,128)(2,1)}, bf16[8,64,384]{2,1,0:T(8,128)(2,1)}, u32[]{:S(2)}, u32[]{:S(2)}) collective-permute-start(bf16[8,64,384]{2,1,0:T(8,128)(2,1)} %pad_maximum_fusion), channel_id=1, source_target_pairs={{0,16},{16,32},{32,48},{48,0},{64,80},{80,96},{96,112},{112,64},{1... | collective-permute-start | bytes 1179656 | tf_op jit(solution)/shard_map/ppermute | solution.py:24
  134.7 7.5 %collective-permute-start.8 = (bf16[8,384,128]{2,1,0:T(8,128)(2,1)}, bf16[8,384,128]{2,1,0:T(8,128)(2,1)S(1)}, u32[]{:S(2)}, u32[]{:S(2)}) collective-permute-start(bf16[8,384,128]{2,1,0:T(8,128)(2,1)} %bitcast.90), channel_id=1, source_target_pairs={{0,1},{1,0},{2,3},{3,2},{4,5},{5,4},{6,7},{7,6},{8,9},{9,8},{10,11... | collective-permute-start | bytes 2359304 | tf_op jit(solution)/shard_map/ppermute | solution.py:29
  138.8 19.0 %all-to-all-start.3 = ((bf16[8,64,384]{2,1,0:T(8,128)(2,1)}), bf16[8,64,384]{2,1,0:T(8,128)(2,1)S(1)}, u32[]{:S(2)}, u32[]{:S(2)}) async-start(bf16[8,64,384]{2,1,0:T(8,128)(2,1)} %fusion.9), calls=%async_computation.3 | async-start | bytes 786432 | tf_op jit(solution)/shard_map/all_to_all | solution.py:99
  157.8 30.4 %all-to-all-start.2 = ((bf16[8,384,128]{2,1,0:T(8,128)(2,1)}), bf16[8,384,128]{2,1,0:T(8,128)(2,1)S(1)}, u32[]{:S(2)}, u32[]{:S(2)}) async-start(bf16[8,384,128]{2,1,0:T(8,128)(2,1)} %fusion), calls=%async_computation.2 | async-start | bytes 1572864 | tf_op jit(solution)/shard_map/all_to_all | solution.py:116
  (1 other events, 3.5 us)
Sparse Core Ops, SparseCore 0:
  10.1 52.2 all-gather.1
where the time goes:
time: 197 us; the launch traced here: 196 us
  waiting for transfers between devices  90.2 us (46%)
  starting transfers between devices  62.9 us (32%)
  between operations  14.6 us (7%)
  local copies, waits for them, and re-layouts  11.9 us (6%)
  matrix products  8.78 us (4%)
  other arithmetic  7.37 us (4%)
    ppermute x12, starting transfers between devices, send_x(): return lax.ppermute(value, 'fsdp', pairs)  36.5 us
    ppermute x12, waiting for transfers between devices, send_x(): return lax.ppermute(value, 'fsdp', pairs)  34.7 us
    all_to_all x1, waiting for transfers between devices, on_device(): summed = lax.all_to_all(pair_sum, 'mp', 0, 0, axis_index_groups=Y_GROUPS)  22.7 us
    all_to_all x2, waiting for transfers between devices, gather_z(): return lax.all_to_all(copies, 'fsdp', 0, 0, axis_index_groups=Z_GROUPS)  18.5 us
    all_to_all x1, waiting for transfers between devices, on_device(): lax.all_to_all(down_x.astype(jnp.bfloat16), 'fsdp', 0, 0, axis_index_grou...  14.3 us
    all_to_all x2, starting transfers between devices, gather_z(): return lax.all_to_all(copies, 'fsdp', 0, 0, axis_index_groups=Z_GROUPS)  13.9 us
    dot_general x6, matrix products, dot(): lax.dot_general(left, right, (dims, ((), ())), preferred_element_type=jnp...  8.78 us
    all_to_all x1, starting transfers between devices, on_device(): summed = lax.all_to_all(pair_sum, 'mp', 0, 0, axis_index_groups=Y_GROUPS)  7.1 us
  transfers between devices with their start and end apart: 18, of which 10 were waited for; matrix products, arithmetic and copies ran while one was open for 9% of the time, Pallas kernels for 0%

commit v1 on v0

v1 whole, which is shorter than its diff:
```python
import math

import jax
import jax.numpy as jnp
from jax import lax
from jax.sharding import PartitionSpec as P

N_Z = 8
N_X = 4
N_Y = 8
N_CORE = 2
Z_GROUPS = [[z * N_X + x for z in range(N_Z)] for x in range(N_X)]
Y_GROUPS = [[y * N_CORE + c for y in range(N_Y)] for c in range(N_CORE)]


def dot(left, right, dims):
    return lax.dot_general(left, right, (dims, ((), ())), preferred_element_type=jnp.float32)


def send_x(value, step):
    pairs = [
        (z * N_X + x, z * N_X + (x + step) % N_X) for z in range(N_Z) for x in range(N_X)
    ]
    return lax.ppermute(value, "fsdp", pairs)


def send_core(value):
    pairs = [(i, i ^ 1) for i in range(N_Y * N_CORE)]
    return lax.ppermute(value, "mp", pairs)


def gather_z(block):
    copies = jnp.broadcast_to(block[None], (N_Z,) + block.shape)
    return lax.all_to_all(copies, "fsdp", 0, 0, axis_index_groups=Z_GROUPS)


def around_x(own):
    half = own.shape[0] // 2
    from_left = send_x(own, 1)
    from_right = send_x(own, -1)
    far_low = send_x(from_left[:half], 1)
    far_high = send_x(from_right[half:], -1)
    return from_left, from_right, far_low, far_high


def add(left, right):
    return left.astype(jnp.float32) + right.astype(jnp.float32)


def neighbours(me):
    return (me + N_X - 1) % N_X, (me + 1) % N_X, (me + 2) % N_X


def put_x(blocks, me):
    own, from_left, from_right, far_low, far_high = blocks
    n_z, rows, cols = own.shape
    left, right, far = neighbours(me)
    full = jnp.zeros((N_CORE, n_z, N_X // N_CORE, rows, cols), own.dtype)
    for block, x, z in (
        (own, me, 0),
        (from_left, left, 0),
        (from_right, right, 0),
        (far_low, far, 0),
        (far_high, far, n_z // 2),
    ):
        full = lax.dynamic_update_slice(full, block[None, :, None], (x // 2, z, x % 2, 0, 0))
    return full


def scatter_x(partial_value, me):
    half = N_Z // 2
    _, n_z, _, rows, cols = partial_value.shape
    left, right, far = neighbours(me)

    def take(x, low, high):
        return lax.dynamic_slice(
            partial_value, (x // 2, low, x % 2, 0, 0), (1, high - low, 1, rows, cols)
        ).reshape(high - low, rows, cols)

    low = send_x(take(far, 0, half), 1)
    high = send_x(take(far, half, N_Z), -1)
    to_right = jnp.concatenate(
        [add(take(right, 0, half), low).astype(jnp.bfloat16), take(right, half, N_Z)]
    )
    to_left = jnp.concatenate(
        [take(left, 0, half), add(take(left, half, N_Z), high).astype(jnp.bfloat16)]
    )
    from_left = send_x(to_right, 1)
    from_right = send_x(to_left, -1)
    return add(take(me, 0, N_Z), from_left) + from_right.astype(jnp.float32)


def on_device(tokens, cotangent, gate_weight, up_weight, down_weight):
    n_fsdp = lax.axis_size("fsdp")
    rows, width = tokens.shape
    depth, cols = gate_weight.shape
    n_feat = depth * n_fsdp
    factor = 1.0 / math.sqrt(rows * n_fsdp)
    me_x = lax.axis_index("fsdp") % N_X
    core = lax.axis_index("mp") % N_CORE

    stacked = jnp.concatenate([tokens, cotangent])
    own_core = lax.all_gather(stacked, "mp", axis_index_groups=Y_GROUPS, axis=1, tiled=True)
    other_core = send_core(own_core)
    both = jnp.zeros((2 * rows, n_feat), tokens.dtype)
    both = lax.dynamic_update_slice(both, own_core, (0, core * N_Y * width))
    both = lax.dynamic_update_slice(both, other_core, (0, (1 - core) * N_Y * width))
    token_rows, cotangent_rows = both[:rows], both[rows:]

    gate_up = gather_z(jnp.concatenate([gate_weight, up_weight]))
    around = (gate_up,) + around_x(gate_up)
    gate_full = put_x([b[:, :depth] for b in around], me_x).reshape(-1, cols)
    up_full = put_x([b[:, depth:] for b in around], me_x).reshape(-1, cols)

    pieces = down_weight.reshape(4, depth // 4, cols)
    from_left, from_right, far_low, far_high = around_x(pieces)
    left, right, far = neighbours(me_x)
    far_block = jnp.concatenate([far_low, far_high])
    down_x = jnp.zeros((N_X, depth, cols), down_weight.dtype)
    for block, x in ((pieces, me_x), (from_left, left), (from_right, right), (far_block, far)):
        down_x = lax.dynamic_update_slice(down_x, block.reshape(1, depth, cols), (x, 0, 0))
    down_full = lax.all_gather(
        down_x.reshape(N_CORE, -1, cols), "fsdp", axis_index_groups=Z_GROUPS, axis=1, tiled=True
    ).reshape(-1, cols)

    gate_value = dot(token_rows, gate_full, ((1,), (0,)))
    up_value = dot(token_rows, up_full, ((1,), (0,)))
    sigmoid_gate = jax.nn.sigmoid(gate_value)
    hidden = (gate_value * sigmoid_gate * up_value).astype(jnp.bfloat16)

    down_partial = dot(cotangent_rows, hidden, ((0,), (0,))).astype(jnp.bfloat16)
    down_z = scatter_x(down_partial.reshape(N_CORE, N_Z, N_X // N_CORE, depth, cols), me_x)
    down_z = lax.all_to_all(
        down_z.astype(jnp.bfloat16), "fsdp", 0, 0, axis_index_groups=Z_GROUPS
    )
    grad_down = (down_z.astype(jnp.float32).sum(0) * factor).astype(jnp.bfloat16)

    hidden_grad = dot(cotangent_rows, down_full, ((1,), (0,)))
    gate_grad = (
        hidden_grad * up_value * sigmoid_gate * (1.0 + gate_value * (1.0 - sigmoid_gate))
    ).astype(jnp.bfloat16)
    up_grad = (hidden_grad * gate_value * sigmoid_gate).astype(jnp.bfloat16)

    def half_partial(which):
        gate_half = lax.dynamic_index_in_dim(gate_full.reshape(N_CORE, -1, cols), which, 0, False)
        up_half = lax.dynamic_index_in_dim(up_full.reshape(N_CORE, -1, cols), which, 0, False)
        value = dot(gate_grad, gate_half, ((1,), (1,))) + dot(up_grad, up_half, ((1,), (1,)))
        return value.astype(jnp.bfloat16).reshape(rows, N_Y, width).transpose(1, 0, 2)

    from_core = send_core(half_partial(1 - core))
    pair_sum = add(half_partial(core), from_core).astype(jnp.bfloat16)
    summed = lax.all_to_all(pair_sum, "mp", 0, 0, axis_index_groups=Y_GROUPS)
    input_grad = summed.astype(jnp.float32).sum(0).astype(jnp.bfloat16)
    return (input_grad, grad_down)


def solution(mesh):
    placed = P("fsdp", "mp")
    return jax.shard_map(
        on_device,
        mesh=mesh,
        in_specs=(placed,) * 5,
        out_specs=(placed, placed),
        check_vma=False,
    )
```

time: 197 us -> 180 us (0.914)
  waiting for transfers between devices: 90.2 us -> 67.1 us
  other arithmetic: 7.37 us -> 11.3 us
  starting transfers between devices: 62.9 us -> 60.2 us
  local copies, waits for them, and re-layouts: 11.9 us -> 14 us
    ppermute x12, waiting for transfers between devices: 34.7 us -> 12.3 us  [send_x(): return lax.ppermute(value, 'fsdp', pairs)]
    all_gather x1 -> x2, waiting for transfers between devices: 0.02 us -> 18.2 us  [the longest x1 9.81 us: on_device(): lax.all_gather(stacked, 'mp', axis_index_groups=Y_GROUPS, axis=1, tiled=T...]
    all_to_all x2 -> x1, waiting for transfers between devices: 18.5 us -> 11.1 us  [gather_z(): return lax.all_to_all(copies, 'fsdp', 0, 0, axis_index_groups=Z_GROUPS)]
    all_to_all x1, waiting for transfers between devices: 14.3 us -> 7.58 us  [on_device(): lax.all_to_all(down_z.astype(jnp.bfloat16), 'fsdp', 0, 0, axis_index_grou...]
    all_to_all x1, waiting for transfers between devices: 22.7 us -> 18 us  [on_device(): summed = lax.all_to_all(pair_sum, 'mp', 0, 0, axis_index_groups=Y_GROUPS)]
    all_to_all x2 -> x1, starting transfers between devices: 13.9 us -> 10.3 us  [gather_z(): return lax.all_to_all(copies, 'fsdp', 0, 0, axis_index_groups=Z_GROUPS)]
    dynamic_update_slice x10 -> x12, local copies, waits for them, and re-layouts: 1.8 us -> 5.31 us  [the longest x6 4.82 us: put_x(): lax.dynamic_update_slice(full, block[None, :, None], (x // 2, z, x % 2, 0...]
    dynamic_slice x2 -> x0, local copies, waits for them, and re-layouts: 3.29 us -> none  [the longest x1 3.24 us: on_device(): mine = lax.dynamic_index_in_dim(blocks, core, 0, keepdims=False)]
  transfers between devices with their start and end apart: 18 -> 19, of which waited for: 10 -> 9; matrix products, arithmetic and copies ran while one was open for 9% -> 16% of each run, Pallas kernels for 0% -> 0%
where the time goes in v1:
time: 180 us; the launch traced here: 177 us
  waiting for transfers between devices  67.1 us (37%)
  starting transfers between devices  60.2 us (33%)
  between operations  14.8 us (8%)
  local copies, waits for them, and re-layouts  14 us (8%)
  other arithmetic  11.3 us (6%)
  matrix products  9.91 us (6%)
    ppermute x12, starting transfers between devices, send_x(): return lax.ppermute(value, 'fsdp', pairs)  35 us
    all_to_all x1, waiting for transfers between devices, on_device(): summed = lax.all_to_all(pair_sum, 'mp', 0, 0, axis_index_groups=Y_GROUPS)  18 us
    ppermute x12, waiting for transfers between devices, send_x(): return lax.ppermute(value, 'fsdp', pairs)  12.3 us
    all_to_all x1, waiting for transfers between devices, gather_z(): return lax.all_to_all(copies, 'fsdp', 0, 0, axis_index_groups=Z_GROUPS)  11.1 us
    all_to_all x1, starting transfers between devices, gather_z(): return lax.all_to_all(copies, 'fsdp', 0, 0, axis_index_groups=Z_GROUPS)  10.3 us
    dot_general x8, matrix products, dot(): lax.dot_general(left, right, (dims, ((), ())), preferred_element_type=jnp...  9.91 us
    all_gather x1, waiting for transfers between devices, on_device(): lax.all_gather(stacked, 'mp', axis_index_groups=Y_GROUPS, axis=1, tiled=T...  9.81 us
    all_gather x1, waiting for transfers between devices, on_device(): lax.all_gather(down_x.reshape(N_CORE, -1, cols), 'fsdp', axis_index_group...  8.4 us
  transfers between devices with their start and end apart: 19, of which 9 were waited for; matrix products, arithmetic and copies ran while one was open for 16% of the time, Pallas kernels for 0%

profile of v1, /device:TPU:6, one launch (start us, length us, event | category | flops | bytes accessed | tf_op | source)
XLA Modules:
  0.0 177.3 jit_solution(1204665059007718056)
XLA Ops:
  10.7 10.3 %all-to-all-start = ((bf16[8,128,384]{2,1,0:T(8,128)(2,1)}), bf16[8,128,384]{2,1,0:T(8,128)(2,1)}, u32[]{:S(2)}, u32[]{:S(2)}) async-start(bf16[8,128,384]{2,1,0:T(8,128)(2,1)} %broadcast_in_dim.44), calls=%async_computation | async-start | bytes 1572864 | tf_op jit(solution)/shard_map/all_to_all | solution.py:34
  21.0 2.4 %collective-permute-start.1 = (bf16[4,16,384]{2,1,0:T(8,128)(2,1)S(1)}, bf16[4,16,384]{2,1,0:T(8,128)(2,1)S(1)}, u32[]{:S(2)}, u32[]{:S(2)}) collective-permute-start(bf16[4,16,384]{2,1,0:T(8,128)(2,1)S(1)} %bitcast.152), channel_id=1, source_target_pairs={{0,16},{16,32},{32,48},{48,0},{64,80},{80,96},{96,112},{112,64},{1... | collective-permute-start | bytes 147464 | tf_op jit(solution)/shard_map/ppermute | solution.py:24
  23.4 3.5 %collective-permute-start.2 = (bf16[4,16,384]{2,1,0:T(8,128)(2,1)S(1)}, bf16[4,16,384]{2,1,0:T(8,128)(2,1)S(1)}, u32[]{:S(2)}, u32[]{:S(2)}) collective-permute-start(bf16[4,16,384]{2,1,0:T(8,128)(2,1)S(1)} %bitcast.153), channel_id=1, source_target_pairs={{0,48},{16,0},{32,16},{48,32},{64,112},{80,64},{96,80},{112,96},{1... | collective-permute-start | bytes 147464 | tf_op jit(solution)/shard_map/ppermute | solution.py:24
  27.2 3.6 %collective-permute-start.3 = (bf16[2,16,384]{2,1,0:T(8,128)(2,1)S(1)}, bf16[2,16,384]{2,1,0:T(8,128)(2,1)S(1)}, u32[]{:S(2)}, u32[]{:S(2)}) collective-permute-start(bf16[2,16,384]{2,1,0:T(8,128)(2,1)S(1)} %slice.65), channel_id=1, source_target_pairs={{0,16},{16,32},{32,48},{48,0},{64,80},{80,96},{96,112},{112,64},{1... | collective-permute-start | bytes 73736 | tf_op jit(solution)/shard_map/ppermute | solution.py:24
  30.9 2.2 %collective-permute-start.4 = (bf16[2,16,384]{2,1,0:T(8,128)(2,1)S(1)}, bf16[2,16,384]{2,1,0:T(8,128)(2,1)S(1)}, u32[]{:S(2)}, u32[]{:S(2)}) collective-permute-start(bf16[2,16,384]{2,1,0:T(8,128)(2,1)S(1)} %slice.66), channel_id=1, source_target_pairs={{0,48},{16,0},{32,16},{48,32},{64,112},{80,64},{96,80},{112,96},{1... | collective-permute-start | bytes 73736 | tf_op jit(solution)/shard_map/ppermute | solution.py:24
  33.1 11.1 %all-to-all-done = bf16[8,128,384]{2,1,0:T(8,128)(2,1)} async-done(((bf16[8,128,384]{2,1,0:T(8,128)(2,1)}), bf16[8,128,384]{2,1,0:T(8,128)(2,1)}, u32[]{:S(2)}, u32[]{:S(2)}) %all-to-all-start) | async-done | bytes 786464 | tf_op jit(solution)/shard_map/all_to_all | solution.py:34
  44.2 2.4 %collective-permute-start.5 = (bf16[8,128,384]{2,1,0:T(8,128)(2,1)}, bf16[8,128,384]{2,1,0:T(8,128)(2,1)}, u32[]{:S(2)}, u32[]{:S(2)}) collective-permute-start(bf16[8,128,384]{2,1,0:T(8,128)(2,1)} %all-to-all-done), channel_id=1, source_target_pairs={{0,16},{16,32},{32,48},{48,0},{64,80},{80,96},{96,112},{112,64},{1... | collective-permute-start | bytes 2359304 | tf_op jit(solution)/shard_map/ppermute | solution.py:24
  46.6 3.5 %collective-permute-start.6 = (bf16[8,128,384]{2,1,0:T(8,128)(2,1)}, bf16[8,128,384]{2,1,0:T(8,128)(2,1)}, u32[]{:S(2)}, u32[]{:S(2)}) collective-permute-start(bf16[8,128,384]{2,1,0:T(8,128)(2,1)} %all-to-all-done), channel_id=1, source_target_pairs={{0,48},{16,0},{32,16},{48,32},{64,112},{80,64},{96,80},{112,96},{1... | collective-permute-start | bytes 2359304 | tf_op jit(solution)/shard_map/ppermute | solution.py:24
  50.8 9.8 %all-gather.3.cloned.1.call-done = bf16[768,1024]{1,0:T(8,128)(2,1)} async-done(((bf16[768,128]{1,0:T(8,128)(2,1)}), bf16[768,1024]{1,0:T(8,128)(2,1)}) %all-gather.3.cloned.1.call-update) | async-done | bytes 1572880 | tf_op jit(solution)/shard_map/all_gather | solution.py:103
  66.9 3.6 %collective-permute-start.7 = (bf16[4,128,384]{2,1,0:T(8,128)(2,1)S(1)}, bf16[4,128,384]{2,1,0:T(8,128)(2,1)S(1)}, u32[]{:S(2)}, u32[]{:S(2)}) collective-permute-start(bf16[4,128,384]{2,1,0:T(8,128)(2,1)S(1)} %slice.71), channel_id=1, source_target_pairs={{0,16},{16,32},{32,48},{48,0},{64,80},{80,96},{96,112},{112,64},{1... | collective-permute-start | bytes 1179656 | tf_op jit(solution)/shard_map/ppermute | solution.py:24
  71.6 2.2 %collective-permute-start.8 = (bf16[4,128,384]{2,1,0:T(8,128)(2,1)S(1)}, bf16[4,128,384]{2,1,0:T(8,128)(2,1)S(1)}, u32[]{:S(2)}, u32[]{:S(2)}) collective-permute-start(bf16[4,128,384]{2,1,0:T(8,128)(2,1)S(1)} %slice.73), channel_id=1, source_target_pairs={{0,48},{16,0},{32,16},{48,32},{64,112},{80,64},{96,80},{112,96},{1... | collective-permute-start | bytes 1179656 | tf_op jit(solution)/shard_map/ppermute | solution.py:24
  76.4 3.3 %collective-permute-done.7 = bf16[4,128,384]{2,1,0:T(8,128)(2,1)S(1)} collective-permute-done((bf16[4,128,384]{2,1,0:T(8,128)(2,1)S(1)}, bf16[4,128,384]{2,1,0:T(8,128)(2,1)S(1)}, u32[]{:S(2)}, u32[]{:S(2)}) %collective-permute-start.7) | collective-permute-done | bytes 393248 | tf_op jit(solution)/shard_map/ppermute | solution.py:24
  79.7 4.9 %collective-permute-done.8 = bf16[4,128,384]{2,1,0:T(8,128)(2,1)S(1)} collective-permute-done((bf16[4,128,384]{2,1,0:T(8,128)(2,1)S(1)}, bf16[4,128,384]{2,1,0:T(8,128)(2,1)S(1)}, u32[]{:S(2)}, u32[]{:S(2)}) %collective-permute-start.8) | collective-permute-done | bytes 393248 | tf_op jit(solution)/shard_map/ppermute | solution.py:24
  93.7 3.9 %collective-permute-start.12 = (bf16[4,64,384]{2,1,0:T(8,128)(2,1)}, bf16[4,64,384]{2,1,0:T(8,128)(2,1)}, u32[]{:S(2)}, u32[]{:S(2)}) collective-permute-start(bf16[4,64,384]{2,1,0:T(8,128)(2,1)} %get-tuple-element.7), channel_id=1, source_target_pairs={{0,48},{16,0},{32,16},{48,32},{64,112},{80,64},{96,80},{112,96},{1... | collective-permute-start | bytes 589832 | tf_op jit(solution)/shard_map/ppermute | solution.py:24
  97.7 8.4 %all-gather.5.cloned.1.call-done = bf16[2,1024,384]{2,1,0:T(8,128)(2,1)} async-done(((bf16[2,128,384]{2,1,0:T(8,128)(2,1)}), bf16[2,1024,384]{2,1,0:T(8,128)(2,1)}) %all-gather.5.cloned.1.call-update) | async-done | bytes 1572880 | tf_op jit(solution)/shard_map/all_gather | solution.py:122
  106.1 3.3 %multiply_convert_fusion.1 = (bf16[384,384]{1,0:T(8,128)(2,1)S(1)}, bf16[384,384]{1,0:T(8,128)(2,1)S(1)}) fusion(f32[384,384]{1,0:T(8,128)} %copy-done.9, f32[384,384]{1,0:T(8,128)} %copy-done.8, bf16[2048,384]{1,0:T(8,128)(2,1)} %bitcast.154, bf16[768,2048]{1,0:T(8,128)(2,1)} %copy-done), kind=kOutput, calls=%fused_computation.31 | convolution fusion | flops 605896704 | bytes 4915200 | tf_op jit(solution)/shard_map/dot_general | solution.py:17
  111.7 2.4 %collective-permute-start.11 = (bf16[8,64,384]{2,1,0:T(8,128)(2,1)}, bf16[8,64,384]{2,1,0:T(8,128)(2,1)}, u32[]{:S(2)}, u32[]{:S(2)}) collective-permute-start(bf16[8,64,384]{2,1,0:T(8,128)(2,1)} %pad_maximum_fusion), channel_id=1, source_target_pairs={{0,16},{16,32},{32,48},{48,0},{64,80},{80,96},{96,112},{112,64},{1... | collective-permute-start | bytes 1179656 | tf_op jit(solution)/shard_map/ppermute | solution.py:24
  114.9 3.4 %collective-permute-start.13 = (bf16[8,64,384]{2,1,0:T(8,128)(2,1)}, bf16[8,64,384]{2,1,0:T(8,128)(2,1)S(1)}, u32[]{:S(2)}, u32[]{:S(2)}) collective-permute-start(bf16[8,64,384]{2,1,0:T(8,128)(2,1)} %pad_maximum_fusion.1), channel_id=1, source_target_pairs={{0,48},{16,0},{32,16},{48,32},{64,112},{80,64},{96,80},{112,96},{1... | collective-permute-start | bytes 1179656 | tf_op jit(solution)/shard_map/ppermute | solution.py:24
  122.6 3.4 %collective-permute-done.13 = bf16[8,64,384]{2,1,0:T(8,128)(2,1)S(1)} collective-permute-done((bf16[8,64,384]{2,1,0:T(8,128)(2,1)}, bf16[8,64,384]{2,1,0:T(8,128)(2,1)S(1)}, u32[]{:S(2)}, u32[]{:S(2)}) %collective-permute-start.13) | collective-permute-done | bytes 393248 | tf_op jit(solution)/shard_map/ppermute | solution.py:24
  128.0 4.2 %all-to-all-start.2 = ((bf16[8,64,384]{2,1,0:T(8,128)(2,1)}), bf16[8,64,384]{2,1,0:T(8,128)(2,1)S(1)}, u32[]{:S(2)}, u32[]{:S(2)}) async-start(bf16[8,64,384]{2,1,0:T(8,128)(2,1)} %fusion.11), calls=%async_computation.2 | async-start | bytes 786432 | tf_op jit(solution)/shard_map/all_to_all | solution.py:133
  134.5 2.2 %fusion.1 = bf16[8,384,128]{2,1,0:T(8,128)(2,1)} fusion(f32[48,8,8,128]{3,2,1,0:T(8,128)S(1)} %convert_bitcast_fusion, bf16[8,384,128]{2,1,0:T(8,128)(2,1)} %collective-permute-done.9), kind=kLoop, calls=%fused_computation.3 | loop fusion | flops 1179648 | bytes 3145728 | tf_op jit(solution)/shard_map/convert_element_type | solution.py:151
  136.7 7.6 %all-to-all-done.2 = bf16[8,64,384]{2,1,0:T(8,128)(2,1)S(1)} async-done(((bf16[8,64,384]{2,1,0:T(8,128)(2,1)}), bf16[8,64,384]{2,1,0:T(8,128)(2,1)S(1)}, u32[]{:S(2)}, u32[]{:S(2)}) %all-to-all-start.2) | async-done | bytes 393248 | tf_op jit(solution)/shard_map/all_to_all | solution.py:133
  144.3 6.7 %all-to-all-start.1 = ((bf16[8,384,128]{2,1,0:T(8,128)(2,1)}), bf16[8,384,128]{2,1,0:T(8,128)(2,1)S(1)}, u32[]{:S(2)}, u32[]{:S(2)}) async-start(bf16[8,384,128]{2,1,0:T(8,128)(2,1)} %fusion.1), calls=%async_computation.1 | async-start | bytes 1572864 | tf_op jit(solution)/shard_map/all_to_all | solution.py:152
  151.7 18.0 %all-to-all-done.1 = bf16[8,384,128]{2,1,0:T(8,128)(2,1)S(1)} async-done(((bf16[8,384,128]{2,1,0:T(8,128)(2,1)}), bf16[8,384,128]{2,1,0:T(8,128)(2,1)S(1)}, u32[]{:S(2)}, u32[]{:S(2)}) %all-to-all-start.1) | async-done | bytes 786464 | tf_op jit(solution)/shard_map/all_to_all | solution.py:152
  (78 shorter events, 36.2 us)
Async XLA Ops:
  7.2 13.9 %copy-start.7 = (bf16[64,384]{1,0:T(8,128)(2,1)S(1)}, bf16[64,384]{1,0:T(8,128)(2,1)}, u32[]{:S(2)}) copy-start(bf16[64,384]{1,0:T(8,128)(2,1)} %param.9) | copy-start | bytes 147460
  7.2 53.5 %all-gather.3.cloned.1.call-start = ((), (), s32[]{:S(2)}) async-start(), calls=%async_computation.3 | async-start | bytes 1769472 | tf_op jit(solution)/shard_map/all_gather | solution.py:103
  10.7 33.5 %all-to-all-start = ((bf16[8,128,384]{2,1,0:T(8,128)(2,1)}), bf16[8,128,384]{2,1,0:T(8,128)(2,1)}, u32[]{:S(2)}, u32[]{:S(2)}) async-start(bf16[8,128,384]{2,1,0:T(8,128)(2,1)} %broadcast_in_dim.44), calls=%async_computation | async-start | bytes 1572864 | tf_op jit(solution)/shard_map/all_to_all | solution.py:34
  21.0 85.1 %all-gather.5.cloned.1.call-start = ((), (), s32[]{:S(2)}) async-start(), calls=%async_computation.4 | async-start | bytes 1769472 | tf_op jit(solution)/shard_map/all_gather | solution.py:122
  21.0 6.2 %collective-permute-start.1 = (bf16[4,16,384]{2,1,0:T(8,128)(2,1)S(1)}, bf16[4,16,384]{2,1,0:T(8,128)(2,1)S(1)}, u32[]{:S(2)}, u32[]{:S(2)}) collective-permute-start(bf16[4,16,384]{2,1,0:T(8,128)(2,1)S(1)} %bitcast.152), channel_id=1, source_target_pairs={{0,16},{16,32},{32,48},{48,0},{64,80},{80,96},{96,112},{112,64},{1... | collective-permute-start | bytes 147464 | tf_op jit(solution)/shard_map/ppermute | solution.py:24
  23.4 7.4 %collective-permute-start.2 = (bf16[4,16,384]{2,1,0:T(8,128)(2,1)S(1)}, bf16[4,16,384]{2,1,0:T(8,128)(2,1)S(1)}, u32[]{:S(2)}, u32[]{:S(2)}) collective-permute-start(bf16[4,16,384]{2,1,0:T(8,128)(2,1)S(1)} %bitcast.153), channel_id=1, source_target_pairs={{0,48},{16,0},{32,16},{48,32},{64,112},{80,64},{96,80},{112,96},{1... | collective-permute-start | bytes 147464 | tf_op jit(solution)/shard_map/ppermute | solution.py:24
  27.2 22.9 %collective-permute-start.3 = (bf16[2,16,384]{2,1,0:T(8,128)(2,1)S(1)}, bf16[2,16,384]{2,1,0:T(8,128)(2,1)S(1)}, u32[]{:S(2)}, u32[]{:S(2)}) collective-permute-start(bf16[2,16,384]{2,1,0:T(8,128)(2,1)S(1)} %slice.65), channel_id=1, source_target_pairs={{0,16},{16,32},{32,48},{48,0},{64,80},{80,96},{96,112},{112,64},{1... | collective-permute-start | bytes 73736 | tf_op jit(solution)/shard_map/ppermute | solution.py:24
  30.9 19.2 %collective-permute-start.4 = (bf16[2,16,384]{2,1,0:T(8,128)(2,1)S(1)}, bf16[2,16,384]{2,1,0:T(8,128)(2,1)S(1)}, u32[]{:S(2)}, u32[]{:S(2)}) collective-permute-start(bf16[2,16,384]{2,1,0:T(8,128)(2,1)S(1)} %slice.66), channel_id=1, source_target_pairs={{0,48},{16,0},{32,16},{48,32},{64,112},{80,64},{96,80},{112,96},{1... | collective-permute-start | bytes 73736 | tf_op jit(solution)/shard_map/ppermute | solution.py:24
  44.2 21.7 %collective-permute-start.5 = (bf16[8,128,384]{2,1,0:T(8,128)(2,1)}, bf16[8,128,384]{2,1,0:T(8,128)(2,1)}, u32[]{:S(2)}, u32[]{:S(2)}) collective-permute-start(bf16[8,128,384]{2,1,0:T(8,128)(2,1)} %all-to-all-done), channel_id=1, source_target_pairs={{0,16},{16,32},{32,48},{48,0},{64,80},{80,96},{96,112},{112,64},{1... | collective-permute-start | bytes 2359304 | tf_op jit(solution)/shard_map/ppermute | solution.py:24
  46.6 23.9 %collective-permute-start.6 = (bf16[8,128,384]{2,1,0:T(8,128)(2,1)}, bf16[8,128,384]{2,1,0:T(8,128)(2,1)}, u32[]{:S(2)}, u32[]{:S(2)}) collective-permute-start(bf16[8,128,384]{2,1,0:T(8,128)(2,1)} %all-to-all-done), channel_id=1, source_target_pairs={{0,48},{16,0},{32,16},{48,32},{64,112},{80,64},{96,80},{112,96},{1... | collective-permute-start | bytes 2359304 | tf_op jit(solution)/shard_map/ppermute | solution.py:24
  60.7 25.6 %collective-permute-start = (bf16[768,1024]{1,0:T(8,128)(2,1)}, bf16[768,1024]{1,0:T(8,128)(2,1)S(1)}, u32[]{:S(2)}, u32[]{:S(2)}) collective-permute-start(bf16[768,1024]{1,0:T(8,128)(2,1)} %all-gather.3.cloned.1.call-done), channel_id=1, source_target_pairs={{0,1},{1,0},{2,3},{3,2},{4,5},{5,4},{6,7},{7,6},{8,9},{9,8},{10,11... | collective-permute-start | bytes 4718600 | tf_op jit(solution)/shard_map/ppermute | solution.py:29
  66.9 12.8 %collective-permute-start.7 = (bf16[4,128,384]{2,1,0:T(8,128)(2,1)S(1)}, bf16[4,128,384]{2,1,0:T(8,128)(2,1)S(1)}, u32[]{:S(2)}, u32[]{:S(2)}) collective-permute-start(bf16[4,128,384]{2,1,0:T(8,128)(2,1)S(1)} %slice.71), channel_id=1, source_target_pairs={{0,16},{16,32},{32,48},{48,0},{64,80},{80,96},{96,112},{112,64},{1... | collective-permute-start | bytes 1179656 | tf_op jit(solution)/shard_map/ppermute | solution.py:24
  71.6 13.0 %collective-permute-start.8 = (bf16[4,128,384]{2,1,0:T(8,128)(2,1)S(1)}, bf16[4,128,384]{2,1,0:T(8,128)(2,1)S(1)}, u32[]{:S(2)}, u32[]{:S(2)}) collective-permute-start(bf16[4,128,384]{2,1,0:T(8,128)(2,1)S(1)} %slice.73), channel_id=1, source_target_pairs={{0,48},{16,0},{32,16},{48,32},{64,112},{80,64},{96,80},{112,96},{1... | collective-permute-start | bytes 1179656 | tf_op jit(solution)/shard_map/ppermute | solution.py:24
  86.5 2.0 %copy-start = (bf16[768,2048]{1,0:T(8,128)(2,1)}, bf16[768,2048]{1,0:T(8,128)(2,1)S(1)}, u32[]{:S(2)}) copy-start(bf16[768,2048]{1,0:T(8,128)(2,1)S(1)} %constant_dynamic-update-slice_fusion) | copy-start | bytes 9437188
  91.8 17.5 %collective-permute-start.10 = (bf16[4,64,384]{2,1,0:T(8,128)(2,1)}, bf16[4,64,384]{2,1,0:T(8,128)(2,1)}, u32[]{:S(2)}, u32[]{:S(2)}) collective-permute-start(bf16[4,64,384]{2,1,0:T(8,128)(2,1)} %get-tuple-element.4), channel_id=1, source_target_pairs={{0,16},{16,32},{32,48},{48,0},{64,80},{80,96},{96,112},{112,64},{1... | collective-permute-start | bytes 589832 | tf_op jit(solution)/shard_map/ppermute | solution.py:24
  93.7 15.6 %collective-permute-start.12 = (bf16[4,64,384]{2,1,0:T(8,128)(2,1)}, bf16[4,64,384]{2,1,0:T(8,128)(2,1)}, u32[]{:S(2)}, u32[]{:S(2)}) collective-permute-start(bf16[4,64,384]{2,1,0:T(8,128)(2,1)} %get-tuple-element.7), channel_id=1, source_target_pairs={{0,48},{16,0},{32,16},{48,32},{64,112},{80,64},{96,80},{112,96},{1... | collective-permute-start | bytes 589832 | tf_op jit(solution)/shard_map/ppermute | solution.py:24
  109.3 9.6 %copy-start.5 = (bf16[384,384]{1,0:T(8,128)(2,1)}, bf16[384,384]{1,0:T(8,128)(2,1)S(1)}, u32[]{:S(2)}) copy-start(bf16[384,384]{1,0:T(8,128)(2,1)S(1)} %get-tuple-element.9) | copy-start | bytes 884740
  109.4 9.6 %copy-start.3 = (bf16[384,384]{1,0:T(8,128)(2,1)}, bf16[384,384]{1,0:T(8,128)(2,1)S(1)}, u32[]{:S(2)}) copy-start(bf16[384,384]{1,0:T(8,128)(2,1)S(1)} %get-tuple-element.8) | copy-start | bytes 884740
  111.7 10.9 %collective-permute-start.11 = (bf16[8,64,384]{2,1,0:T(8,128)(2,1)}, bf16[8,64,384]{2,1,0:T(8,128)(2,1)}, u32[]{:S(2)}, u32[]{:S(2)}) collective-permute-start(bf16[8,64,384]{2,1,0:T(8,128)(2,1)} %pad_maximum_fusion), channel_id=1, source_target_pairs={{0,16},{16,32},{32,48},{48,0},{64,80},{80,96},{96,112},{112,64},{1... | collective-permute-start | bytes 1179656 | tf_op jit(solution)/shard_map/ppermute | solution.py:24
  114.9 11.1 %collective-permute-start.13 = (bf16[8,64,384]{2,1,0:T(8,128)(2,1)}, bf16[8,64,384]{2,1,0:T(8,128)(2,1)S(1)}, u32[]{:S(2)}, u32[]{:S(2)}) collective-permute-start(bf16[8,64,384]{2,1,0:T(8,128)(2,1)} %pad_maximum_fusion.1), channel_id=1, source_target_pairs={{0,48},{16,0},{32,16},{48,32},{64,112},{80,64},{96,80},{112,96},{1... | collective-permute-start | bytes 1179656 | tf_op jit(solution)/shard_map/ppermute | solution.py:24
  120.6 13.8 %collective-permute-start.9 = (bf16[8,384,128]{2,1,0:T(8,128)(2,1)}, bf16[8,384,128]{2,1,0:T(8,128)(2,1)}, u32[]{:S(2)}, u32[]{:S(2)}) collective-permute-start(bf16[8,384,128]{2,1,0:T(8,128)(2,1)} %bitcast.135), channel_id=1, source_target_pairs={{0,1},{1,0},{2,3},{3,2},{4,5},{5,4},{6,7},{7,6},{8,9},{9,8},{10,11... | collective-permute-start | bytes 2359304 | tf_op jit(solution)/shard_map/ppermute | solution.py:29
  128.0 16.3 %all-to-all-start.2 = ((bf16[8,64,384]{2,1,0:T(8,128)(2,1)}), bf16[8,64,384]{2,1,0:T(8,128)(2,1)S(1)}, u32[]{:S(2)}, u32[]{:S(2)}) async-start(bf16[8,64,384]{2,1,0:T(8,128)(2,1)} %fusion.11), calls=%async_computation.2 | async-start | bytes 786432 | tf_op jit(solution)/shard_map/all_to_all | solution.py:133
  132.2 1.6 copy-start.4
  144.3 25.4 %all-to-all-start.1 = ((bf16[8,384,128]{2,1,0:T(8,128)(2,1)}), bf16[8,384,128]{2,1,0:T(8,128)(2,1)S(1)}, u32[]{:S(2)}, u32[]{:S(2)}) async-start(bf16[8,384,128]{2,1,0:T(8,128)(2,1)} %fusion.1), calls=%async_computation.1 | async-start | bytes 1572864 | tf_op jit(solution)/shard_map/all_to_all | solution.py:152
  (5 other events, 5.5 us)
Sparse Core Ops, SparseCore 0:
  10.0 50.5 all-gather.2
  62.7 43.2 all-gather.4
